TPU v7x, 32 devices: a whole 2x2x4 slice. The times are simulated.
32 devices in a mesh: blk: 4 (over y, x), mode: 8 (over z, core).
Axes of the slice: x: 2, y: 2, z: 4, core: 2. Of those that a mesh axis runs over, the one named last changes fastest.
Arguments:
- density: bfloat16 [2, 128, 1024, 256], P(None, 'mode', 'blk'), may hold values from -6 to 6
- kernel_tiles: bfloat16 [128, 8, 4, 2, 128, 128], P('mode', 'blk'), may hold values from -0.1875 to 0.1875
- tile_index: int32 [128, 8, 4], P('mode', 'blk'), may hold values from 0 to 1
- coupling: bfloat16 [2, 9, 128, 1024], P(None, None, 'mode', 'blk'), may hold values from -4 to 4
- spread: int32 [1024], P('blk'), may hold values from 0 to 4
- liner: int32 [1024], P('blk'), may hold values 0 or 1
Outputs:
- applied: bfloat16 [2, 128, 1024, 256], P(None, 'mode', 'blk')
Inputs may be any that keep to these rules, and one draw needn't show every extreme that they name: `tile_index`: each retained tile names one column tile of its source shard.
All inputs are finite; a program needn't handle non-finite values. No bound on the sum of `liner` on one device may be relied on, other than what follows from the above.
Results may differ from a plain program's by a relative error of at most 0.0033.
Values may be sent and summed in bfloat16 or wider, within the bound.
A program may use at most 320 MiB of HBM per device.

v0:
```python
import jax
import jax.numpy as jnp
from jax import lax
from jax.sharding import PartitionSpec as P


def with_halo(block, sides, width):
    for axis, dim in sides:
        count = lax.axis_size(axis)
        forward = [(i, i + 1) for i in range(count - 1)]
        backward = [(target, source) for source, target in forward]
        low = lax.ppermute(
            lax.slice_in_dim(block, block.shape[dim] - width, None, axis=dim), axis, forward
        )
        high = lax.ppermute(lax.slice_in_dim(block, 0, width, axis=dim), axis, backward)
        block = jnp.concatenate([low, block, high], axis=dim)
    return block


def tile_product(left, right):
    return jnp.einsum("mtqk,mtkr->mtqr", left, right, preferred_element_type=jnp.float32)


def couple_modes(padded, weights, mode_count):
    band_count = weights.shape[1]
    real_part = jnp.zeros((mode_count,) + padded.shape[2:], jnp.float32)
    imag_part = jnp.zeros((mode_count,) + padded.shape[2:], jnp.float32)
    for offset in range(band_count):
        shifted = padded[:, offset : offset + mode_count].astype(jnp.float32)
        weight_now = weights[:, offset].astype(jnp.float32)[..., None]
        real_part = real_part + weight_now[0] * shifted[0] - weight_now[1] * shifted[1]
        imag_part = imag_part + weight_now[0] * shifted[1] + weight_now[1] * shifted[0]
    return jnp.stack([real_part, imag_part]).astype(jnp.bfloat16)


def shards(density, kernel_tiles, tile_index, coupling, spread, liner):
    mode_count = density.shape[1]
    point_count = density.shape[2]
    rhs_count = density.shape[3]
    tile_size = kernel_tiles.shape[-1]
    row_tiles = kernel_tiles.shape[1]
    per_shard = point_count // tile_size
    band_count = coupling.shape[1]
    reach = band_count // 2
    column_ids = jnp.arange(per_shard, dtype=jnp.int32)
    initial = jnp.zeros((2, mode_count, row_tiles, tile_size, rhs_count), jnp.float32)
    gathered = lax.all_gather(density, "blk", axis=2, tiled=True)
    shard_count = gathered.shape[2] // point_count

    def one_shard(position, running):
        shard_block = lax.dynamic_slice_in_dim(gathered, position * point_count, point_count, 2)
        shard_block = shard_block.reshape(2, mode_count, per_shard, tile_size, rhs_count)
        chosen_tiles = lax.dynamic_index_in_dim(tile_index, position, 2, keepdims=False)
        one_hot = (chosen_tiles[:, :, None] == column_ids).astype(jnp.bfloat16)
        picked_tiles = jnp.einsum(
            "mts,cmsqr->cmtqr", one_hot, shard_block, preferred_element_type=jnp.float32
        ).astype(jnp.bfloat16)
        kernel_block = lax.dynamic_index_in_dim(kernel_tiles, position, 2, keepdims=False)
        real_part = tile_product(kernel_block[:, :, 0], picked_tiles[0]) - tile_product(
            kernel_block[:, :, 1], picked_tiles[1]
        )
        imag_part = tile_product(kernel_block[:, :, 0], picked_tiles[1]) + tile_product(
            kernel_block[:, :, 1], picked_tiles[0]
        )
        return running + jnp.stack([real_part, imag_part])

    near = lax.fori_loop(0, shard_count, one_shard, initial)
    near = near.reshape(2, mode_count, point_count, rhs_count)
    offsets = jnp.abs(jnp.arange(band_count, dtype=jnp.int32) - reach)
    within = (offsets[:, None] <= spread[None, :]) & (liner[None, :] == 1)
    weights = coupling * within[None, :, None, :].astype(jnp.bfloat16)
    extended = with_halo(density, (("mode", 1),), reach)
    coupled = couple_modes(extended, weights, mode_count)
    total = 0.5 * density.astype(jnp.float32) + near + coupled.astype(jnp.float32)
    return total.astype(jnp.bfloat16)


def solution(mesh):
    return jax.shard_map(
        shards,
        mesh=mesh,
        in_specs=(
            P(None, "mode", "blk", None),
            P("mode", "blk", None, None, None, None),
            P("mode", "blk", None),
            P(None, None, "mode", "blk"),
            P("blk"),
            P("blk"),
        ),
        out_specs=P(None, "mode", "blk", None),
        check_vma=False,
    )
```

profile of v0, /device:TPU:0, one launch (start us, length us, event | category | flops | bytes accessed | tf_op | source)
XLA Modules:
  0.0 355.8 jit_solution(15643037743897326441)
XLA Ops:
  7.3 3.1 fusion.14
  15.2 9.4 %constant_dynamic-update-slice_fusion = (bf16[2,20,256,256]{3,2,1,0:T(8,128)(2,1)S(1)}, f32[2,16,256,256]{3,2,1,0:T(8,128)}, bf16[2,20,256,256]{3,2,1,0:T(8,128)(2,1)S(1)}) fusion(bf16[2,20,256,256]{3,2,1,0:T(8,128)(2,1)S(1)} %constant_dynamic-update-slice_fusion.1, bf16[2,16,256,256]{3,2,1,0:T(8,128)(2,1)} %param.8), kind=kLoop, calls=%fused_computation.66 | loop fusion | flops 2097151 | bytes 20971520 | tf_op jit(solution)/shard_map/concatenate | solution.py:16
  24.7 2.9 copy-done
  27.7 11.7 %slice_convert_fusion.3 = (f32[2,16,256,256]{3,2,1,0:T(8,128)}, f32[2,16,256,256]{3,2,1,0:T(8,128)}, f32[2,16,256,256]{3,2,1,0:T(8,128)}, f32[2,16,256,256]{3,2,1,0:T(8,128)}) fusion(bf16[2,20,256,256]{3,2,1,0:T(8,128)(2,1)S(1)} %constant_dynamic-update-slice_fusion.2), kind=kLoop, calls=%fused_computation.30 | loop fusion | flops 8388608 | bytes 50331648 | tf_op jit(solution)/shard_map/convert_element_type | solution.py:29
  39.4 15.3 %slice_convert_fusion.7 = (f32[2,16,256,256]{3,2,1,0:T(8,128)}, f32[2,16,256,256]{3,2,1,0:T(8,128)}, f32[2,16,256,256]{3,2,1,0:T(8,128)}, f32[2,16,256,256]{3,2,1,0:T(8,128)}) fusion(bf16[2,20,256,256]{3,2,1,0:T(8,128)(2,1)} %copy-done), kind=kLoop, calls=%fused_computation.34 | loop fusion | flops 8388608 | bytes 50331648 | tf_op jit(solution)/shard_map/convert_element_type | solution.py:29
  54.6 25.1 %subtract_convert_fusion = bf16[1,16,256,256]{3,2,1,0:T(8,128)(2,1)} fusion(f32[2,16,256,256]{3,2,1,0:T(8,128)} %get-tuple-element.162, f32[2,16,256,256]{3,2,1,0:T(8,128)} %get-tuple-element.163, f32[2,16,256,256]{3,2,1,0:T(8,128)} %get-tuple-element.164, f32[2,16,256,256]{3,2,1,0:T(8,128)} %get-tuple-element.161, ...), kind=kLoop, calls=%fused_computation.36 | loop fusion | flops 37748736 | bytes 77889536 | tf_op jit(solution)/shard_map/convert
  79.8 25.7 %add_convert_fusion = bf16[1,16,256,256]{3,2,1,0:T(8,128)(2,1)} fusion(f32[2,16,256,256]{3,2,1,0:T(8,128)} %get-tuple-element.162, f32[2,16,256,256]{3,2,1,0:T(8,128)} %get-tuple-element.163, f32[2,16,256,256]{3,2,1,0:T(8,128)} %get-tuple-element.164, f32[2,16,256,256]{3,2,1,0:T(8,128)} %get-tuple-element.161, f32[2,16,256,256]{3,2,1,0:T(8,128)} %get-tuple-element.166, ...), kind=kLoop, calls=%fused_computation.35 | loop fusion | flops 37748736 | bytes 77889536 | tf_op jit(solution)/shard_map/convert.1
  105.5 63.9 %all-gather.2.cloned.1.call-done = bf16[2,16,1024,256]{3,2,1,0:T(8,128)(2,1)} async-done(((bf16[2,16,256,256]{3,2,1,0:T(8,128)(2,1)}), bf16[2,16,1024,256]{3,2,1,0:T(8,128)(2,1)}) %all-gather.2.cloned.1.call-update) | async-done | bytes 16777232 | tf_op jit(solution)/shard_map/all_gather | solution.py:47
  169.4 171.7 %while.14 = (s32[]{:T(128)}, f32[2,16,2,128,256]{4,3,2,1,0:T(8,128)}, bf16[16,2,4,2,128,128]{5,4,3,2,1,0:T(8,128)(2,1)}, bf16[2,16,1024,256]{3,2,1,0:T(8,128)(2,...) while((s32[]{:T(128)}, f32[2,16,2,128,256]{4,3,2,1,0:T(8,128)}, ...), condition=%wide.region_1.2_spmd.clone, body=%wide.region_0.1_spmd.clone.sunk | while | flops 1092616192 | bytes 92275992 | solution.py:67
  169.4 4.8 %constant_dynamic-slice_fusion.8 = bf16[2,16,256,256]{3,2,1,0:T(8,128)(2,1)} fusion(bf16[2,16,1024,256]{3,2,1,0:T(8,128)(2,1)} %get-tuple-element.261, s32[]{:T(128)S(6)} %select_n.17), kind=kLoop, calls=%fused_computation.22.clone.1 | loop fusion | bytes 8388612 | tf_op jit(solution)/shard_map/while/body/eval_jaxpr/dynamic_slice | solution.py:51
  174.9 16.7 %fusion.28 = bf16[2,16,2,128,256]{4,2,3,0,1:T(2,128)(2,1)S(1)} fusion(bf16[2,16,2,128,256]{4,3,2,1,0:T(8,128)(2,1)} %bitcast.95, s32[16,2]{1,0:T(8,128)S(1)} %copy.49), kind=kOutput, calls=%fused_computation.3.clone.1 | convolution fusion | flops 10485824 | bytes 8388736 | tf_op jit(solution)/shard_map/while/body/eval_jaxpr/mts,cmsqr->cmtqr/dot_general | solution.py:55
  191.7 3.0 slice_bitcast_fusion.35
  200.6 2.7 add_bitcast_fusion.2
  203.3 6.3 %maximum_add_fusion.2 = f32[2,16,2,128,256]{4,3,2,1,0:T(8,128)} fusion(f32[1,16,2,128,256]{4,3,2,1,0:T(8,128)} %add_bitcast_fusion.2, f32[1,16,2,128,256]{4,3,2,1,0:T(8,128)} %subtract_bitcast_fusion.2, f32[2,16,2,128,256]{4,3,2,1,0:T(8,128)} %get-tuple-element.250, pred[]{:T(512)S(6)} %compare.3), kind=kLoop, calls=%fused_computation.1.clone.1 | loop fusion | flops 6291456 | bytes 25165824 | tf_op jit(solution)/shard_map/while/body/eval_jaxpr/add | solution.py:65
  209.5 4.6 %constant_dynamic-slice_fusion.8 = bf16[2,16,256,256]{3,2,1,0:T(8,128)(2,1)} fusion(bf16[2,16,1024,256]{3,2,1,0:T(8,128)(2,1)} %get-tuple-element.261, s32[]{:T(128)S(6)} %select_n.17), kind=kLoop, calls=%fused_computation.22.clone.1 | loop fusion | bytes 8388612 | tf_op jit(solution)/shard_map/while/body/eval_jaxpr/dynamic_slice | solution.py:51
  215.0 16.7 %fusion.28 = bf16[2,16,2,128,256]{4,2,3,0,1:T(2,128)(2,1)S(1)} fusion(bf16[2,16,2,128,256]{4,3,2,1,0:T(8,128)(2,1)} %bitcast.95, s32[16,2]{1,0:T(8,128)S(1)} %copy.49), kind=kOutput, calls=%fused_computation.3.clone.1 | convolution fusion | flops 10485824 | bytes 8388736 | tf_op jit(solution)/shard_map/while/body/eval_jaxpr/mts,cmsqr->cmtqr/dot_general | solution.py:55
  231.7 3.0 slice_bitcast_fusion.35
  237.2 2.7 subtract_bitcast_fusion.2
  240.6 2.7 add_bitcast_fusion.2
  243.3 10.1 %maximum_add_fusion.2 = f32[2,16,2,128,256]{4,3,2,1,0:T(8,128)} fusion(f32[1,16,2,128,256]{4,3,2,1,0:T(8,128)} %add_bitcast_fusion.2, f32[1,16,2,128,256]{4,3,2,1,0:T(8,128)} %subtract_bitcast_fusion.2, f32[2,16,2,128,256]{4,3,2,1,0:T(8,128)} %get-tuple-element.250, pred[]{:T(512)S(6)} %compare.3), kind=kLoop, calls=%fused_computation.1.clone.1 | loop fusion | flops 6291456 | bytes 25165824 | tf_op jit(solution)/shard_map/while/body/eval_jaxpr/add | solution.py:65
  253.4 4.6 %constant_dynamic-slice_fusion.8 = bf16[2,16,256,256]{3,2,1,0:T(8,128)(2,1)} fusion(bf16[2,16,1024,256]{3,2,1,0:T(8,128)(2,1)} %get-tuple-element.261, s32[]{:T(128)S(6)} %select_n.17), kind=kLoop, calls=%fused_computation.22.clone.1 | loop fusion | bytes 8388612 | tf_op jit(solution)/shard_map/while/body/eval_jaxpr/dynamic_slice | solution.py:51
  258.8 16.7 %fusion.28 = bf16[2,16,2,128,256]{4,2,3,0,1:T(2,128)(2,1)S(1)} fusion(bf16[2,16,2,128,256]{4,3,2,1,0:T(8,128)(2,1)} %bitcast.95, s32[16,2]{1,0:T(8,128)S(1)} %copy.49), kind=kOutput, calls=%fused_computation.3.clone.1 | convolution fusion | flops 10485824 | bytes 8388736 | tf_op jit(solution)/shard_map/while/body/eval_jaxpr/mts,cmsqr->cmtqr/dot_general | solution.py:55
  275.5 3.0 slice_bitcast_fusion.35
  281.1 2.7 subtract_bitcast_fusion.2
  284.4 2.7 add_bitcast_fusion.2
  287.2 10.1 %maximum_add_fusion.2 = f32[2,16,2,128,256]{4,3,2,1,0:T(8,128)} fusion(f32[1,16,2,128,256]{4,3,2,1,0:T(8,128)} %add_bitcast_fusion.2, f32[1,16,2,128,256]{4,3,2,1,0:T(8,128)} %subtract_bitcast_fusion.2, f32[2,16,2,128,256]{4,3,2,1,0:T(8,128)} %get-tuple-element.250, pred[]{:T(512)S(6)} %compare.3), kind=kLoop, calls=%fused_computation.1.clone.1 | loop fusion | flops 6291456 | bytes 25165824 | tf_op jit(solution)/shard_map/while/body/eval_jaxpr/add | solution.py:65
  297.2 4.6 %constant_dynamic-slice_fusion.8 = bf16[2,16,256,256]{3,2,1,0:T(8,128)(2,1)} fusion(bf16[2,16,1024,256]{3,2,1,0:T(8,128)(2,1)} %get-tuple-element.261, s32[]{:T(128)S(6)} %select_n.17), kind=kLoop, calls=%fused_computation.22.clone.1 | loop fusion | bytes 8388612 | tf_op jit(solution)/shard_map/while/body/eval_jaxpr/dynamic_slice | solution.py:51
  302.7 16.7 %fusion.28 = bf16[2,16,2,128,256]{4,2,3,0,1:T(2,128)(2,1)S(1)} fusion(bf16[2,16,2,128,256]{4,3,2,1,0:T(8,128)(2,1)} %bitcast.95, s32[16,2]{1,0:T(8,128)S(1)} %copy.49), kind=kOutput, calls=%fused_computation.3.clone.1 | convolution fusion | flops 10485824 | bytes 8388736 | tf_op jit(solution)/shard_map/while/body/eval_jaxpr/mts,cmsqr->cmtqr/dot_general | solution.py:55
  319.4 3.0 slice_bitcast_fusion.35
  328.3 2.7 add_bitcast_fusion.2
  331.0 10.1 %maximum_add_fusion.2 = f32[2,16,2,128,256]{4,3,2,1,0:T(8,128)} fusion(f32[1,16,2,128,256]{4,3,2,1,0:T(8,128)} %add_bitcast_fusion.2, f32[1,16,2,128,256]{4,3,2,1,0:T(8,128)} %subtract_bitcast_fusion.2, f32[2,16,2,128,256]{4,3,2,1,0:T(8,128)} %get-tuple-element.250, pred[]{:T(512)S(6)} %compare.3), kind=kLoop, calls=%fused_computation.1.clone.1 | loop fusion | flops 6291456 | bytes 25165824 | tf_op jit(solution)/shard_map/while/body/eval_jaxpr/add | solution.py:65
  341.1 7.8 %fusion.13 = bf16[2,16,256,256]{3,2,1,0:T(8,128)(2,1)} fusion(f32[2,16,2,128,256]{4,3,2,1,0:T(8,128)} %get-tuple-element.114, bf16[1,16,256,256]{3,2,1,0:T(8,128)(2,1)} %add_convert_fusion, bf16[1,16,256,256]{3,2,1,0:T(8,128)(2,1)S(1)} %copy-done.1, bf16[2,16,256,256]{3,2,1,0:T(8,128)(2,1)} %param.8), kind=kLoop, calls=%fused_computation.26 | loop fusion | flops 14680064 | bytes 20971520 | tf_op jit(solution)/shard_map/convert_element_type | solution.py:75
  (50 shorter events, 27.0 us)
Async XLA Ops:
  6.5 7.5 %copy-start.4 = (s32[256]{0:T(256)S(1)}, s32[256]{0:T(256)}, u32[]{:S(2)}) copy-start(s32[256]{0:T(256)} %param.13) | copy-start | bytes 3076
  6.5 7.6 %copy-start.3 = (s32[256]{0:T(256)S(1)}, s32[256]{0:T(256)}, u32[]{:S(2)}) copy-start(s32[256]{0:T(256)} %param.12) | copy-start | bytes 3076
  6.5 7.7 %copy-start.2 = (bf16[2,9,16,256]{3,2,1,0:T(8,128)(2,1)S(1)}, bf16[2,9,16,256]{3,2,1,0:T(8,128)(2,1)}, u32[]{:S(2)}) copy-start(bf16[2,9,16,256]{3,2,1,0:T(8,128)(2,1)} %param.11) | copy-start | bytes 442372
  6.5 162.8 %all-gather.2.cloned.1.call-start = ((), (), s32[]{:S(2)}) async-start(), calls=%async_computation | async-start | bytes 20971520 | tf_op jit(solution)/shard_map/all_gather | solution.py:47
  10.3 4.8 %collective-permute-start = (bf16[2,4,256,256]{3,2,1,0:T(8,128)(2,1)}, bf16[2,4,256,256]{3,2,1,0:T(8,128)(2,1)S(1)}, u32[]{:S(2)}, u32[]{:S(2)}) collective-permute-start(bf16[2,4,256,256]{3,2,1,0:T(8,128)(2,1)} %get-tuple-element.168), channel_id=1, source_target_pairs={{0,1},{1,2},{2,3},{3,4},{4,5},{5,6},{6,7},{8,9},{9,10},{10,11},{11... | collective-permute-start | bytes 3145736 | tf_op jit(solution)/shard_map/ppermute | solution.py:12
  12.8 11.9 %collective-permute-start.1 = (bf16[2,4,256,256]{3,2,1,0:T(8,128)(2,1)}, bf16[2,4,256,256]{3,2,1,0:T(8,128)(2,1)S(1)}, u32[]{:S(2)}, u32[]{:S(2)}) collective-permute-start(bf16[2,4,256,256]{3,2,1,0:T(8,128)(2,1)} %get-tuple-element.169), channel_id=1, source_target_pairs={{1,0},{2,1},{3,2},{4,3},{5,4},{6,5},{7,6},{9,8},{10,9},{11,10},{12... | collective-permute-start | bytes 3145736 | tf_op jit(solution)/shard_map/ppermute | solution.py:15
  24.7 2.9 copy-start
  169.4 171.7 %copy-start.1 = (bf16[1,16,256,256]{3,2,1,0:T(8,128)(2,1)S(1)}, bf16[1,16,256,256]{3,2,1,0:T(8,128)(2,1)}, u32[]{:S(2)}) copy-start(bf16[1,16,256,256]{3,2,1,0:T(8,128)(2,1)} %subtract_convert_fusion) | copy-start | bytes 6291460
Sparse Core Ops, SparseCore 0:
  9.2 160.1 all-gather.1
where the time goes:
time: 356 us
  other arithmetic  132 us (37%)
  matrix products  94.1 us (26%)
  waiting for transfers between devices  65.5 us (18%)
  local copies, waits for them, and re-layouts  47.2 us (13%)
  between operations  13.5 us (4%)
  starting transfers between devices  3.7 us (1%)
    dot_general x4, matrix products, one_shard(): jnp.einsum('mts,cmsqr->cmtqr', one_hot, shard_block, preferred_element_ty...  66.9 us
    all_gather x1, waiting for transfers between devices, shards(): gathered = lax.all_gather(density, 'blk', axis=2, tiled=True)  63.9 us
    another operation x2, other arithmetic  50.8 us
    add x4, other arithmetic, one_shard(): return running + jnp.stack([real_part, imag_part])  36.5 us
    dot_general x16, matrix products, tile_product(): jnp.einsum('mtqk,mtkr->mtqr', left, right, preferred_element_type=jnp.flo...  27.2 us
    convert_element_type x2, other arithmetic, couple_modes(): shifted = padded[:, offset:offset + mode_count].astype(jnp.float32)  26.9 us
    dynamic_slice x4, local copies, waits for them, and re-layouts, one_shard(): lax.dynamic_slice_in_dim(gathered, position * point_count, point_count, 2)  18.7 us
    squeeze x4, local copies, waits for them, and re-layouts, one_shard(): picked_tiles[0]  11.8 us
  transfers between devices with their start and end apart: 3, of which 2 were waited for; matrix products, arithmetic and copies ran while one was open for 25% of the time, Pallas kernels for 0%

commit v1 on v0

v1 whole, which is shorter than its diff:
```python
import functools

import jax
import jax.numpy as jnp
from jax import lax
from jax.experimental import pallas as pl
from jax.experimental.pallas import tpu as pltpu
from jax.sharding import PartitionSpec as P

F32 = jnp.float32
BF16 = jnp.bfloat16
MIB = 1024 * 1024
ROWS = 32


def operator_kernel(
    cfg, index_ref, spread_ref, liner_ref, coupling_ref, density_ref, tiles_ref, out_ref,
    extended, gathered, tiles, result, coupling32, raw, weights,
    own_sems, forward_sems, arrive_sems, halo_send, halo_arrive, local_sems, out_sems,
):
    shards, groups, step, modes, reach, mode_devices = cfg
    high_count = shards // 2
    band = 2 * reach + 1
    row_tiles = tiles_ref.shape[1]
    tile = tiles_ref.shape[-1]
    points = density_ref.shape[2]
    blk = lax.axis_index("blk")
    mode_at = lax.axis_index("mode")
    high, low = blk // 2, blk % 2
    partner = high * 2 + (1 - low)

    def along(k):
        return lax.rem(high + k, high_count) * 2 + low

    def part(g):
        return pl.ds(g * step, step)

    def own_copy(c, k, g):
        target = partner if k == 0 else along(k)
        slot = 0 if k == 0 else (high_count - k) * 2 - 1
        return pltpu.make_async_remote_copy(
            src_ref=density_ref.at[c, part(g)],
            dst_ref=gathered.at[slot, c, part(g)],
            send_sem=own_sems.at[c, k, g],
            recv_sem=arrive_sems.at[slot, c, g],
            device_id={"blk": target},
        )

    def forward_copy(c, k, g):
        if c == 0:
            source, slot, target = 0, (high_count - k) * 2, along(k)
        else:
            source, slot, target = k * 2 - 1, k * 2, partner
        return pltpu.make_async_remote_copy(
            src_ref=gathered.at[source, c, part(g)],
            dst_ref=gathered.at[slot, c, part(g)],
            send_sem=forward_sems.at[c, k - 1, g],
            recv_sem=arrive_sems.at[slot, c, g],
            device_id={"blk": target},
        )

    def arrived(slot, c, g):
        pltpu.make_async_remote_copy(
            src_ref=gathered.at[slot, c, part(g)],
            dst_ref=gathered.at[slot, c, part(g)],
            send_sem=arrive_sems.at[slot, c, g],
            recv_sem=arrive_sems.at[slot, c, g],
            device_id={"blk": partner},
        ).wait_recv()

    def halo_copy(side):
        source = modes - reach if side == 0 else 0
        target = reach + modes if side == 1 else 0
        neighbour = mode_at + 1 if side == 0 else mode_at - 1
        return pltpu.make_async_remote_copy(
            src_ref=density_ref.at[:, pl.ds(source, reach)],
            dst_ref=extended.at[:, pl.ds(target, reach)],
            send_sem=halo_send.at[side],
            recv_sem=halo_arrive.at[side],
            device_id={"mode": neighbour},
        )

    has_left = mode_at > 0
    has_right = mode_at < mode_devices - 1

    own_load = pltpu.make_async_copy(
        density_ref, extended.at[:, pl.ds(reach, modes)], local_sems.at[0]
    )
    tiles_load = pltpu.make_async_copy(tiles_ref, tiles, local_sems.at[1])
    own_load.start()
    tiles_load.start()

    barrier = pltpu.get_barrier_semaphore()
    pl.semaphore_signal(barrier, inc=1, device_id={"blk": partner})
    for k in range(1, high_count):
        pl.semaphore_signal(barrier, inc=1, device_id={"blk": along(k)})

    @pl.when(has_left)
    def _():
        pl.semaphore_signal(barrier, inc=1, device_id={"mode": mode_at - 1})

    @pl.when(has_right)
    def _():
        pl.semaphore_signal(barrier, inc=1, device_id={"mode": mode_at + 1})

    peers = high_count + jnp.where(has_left, 1, 0) + jnp.where(has_right, 1, 0)
    pl.semaphore_wait(barrier, peers)

    @pl.when(has_right)
    def _():
        halo_copy(0).start()

    @pl.when(has_left)
    def _():
        halo_copy(1).start()

    @pl.loop(0, groups)
    def _(g):
        own_copy(0, 0, g).start()
        for k in range(1, high_count):
            own_copy(1, k, g).start()

    @pl.loop(0, groups)
    def _(g):
        own_copy(1, 0, g).start()
        for k in range(1, high_count):
            own_copy(0, k, g).start()

    coupling32[...] = coupling_ref[...].astype(F32)
    raw[...] = jnp.zeros_like(raw)

    @pl.when(jnp.logical_not(has_left))
    def _():
        extended[:, pl.ds(0, reach)] = jnp.zeros((2, reach) + extended.shape[2:], BF16)

    @pl.when(jnp.logical_not(has_right))
    def _():
        extended[:, pl.ds(reach + modes, reach)] = jnp.zeros((2, reach) + extended.shape[2:], BF16)

    own_load.wait()

    @pl.when(has_left)
    def _():
        halo_copy(0).wait_recv()

    @pl.when(has_right)
    def _():
        halo_copy(1).wait_recv()

    def couple_mode(m):
        on_liner = liner_ref[...] == 1
        reach_of = spread_ref[...]
        for d in range(band):
            inside = jnp.where(on_liner & (reach_of >= abs(d - reach)), 1.0, 0.0).astype(F32)
            for c in range(2):
                raw[pl.ds(c * band + d, 1), :] = coupling32[c, d, pl.ds(m, 1), :] * inside
        weights[...] = jnp.transpose(raw[...])

        @pl.loop(0, points // ROWS)
        def _(b):
            rows = pl.ds(pl.multiple_of(b * ROWS, ROWS), ROWS)
            weight = weights[rows, :]
            real = jnp.zeros((ROWS, extended.shape[3]), F32)
            imag = jnp.zeros((ROWS, extended.shape[3]), F32)
            for d in range(band):
                shifted_r = extended[0, m + d, rows, :].astype(F32)
                shifted_i = extended[1, m + d, rows, :].astype(F32)
                w_r = weight[:, d : d + 1]
                w_i = weight[:, band + d : band + d + 1]
                real = real + w_r * shifted_r - w_i * shifted_i
                imag = imag + w_r * shifted_i + w_i * shifted_r
            result[0, m, rows, :] = real.astype(BF16)
            result[1, m, rows, :] = imag.astype(BF16)

    @pl.loop(0, groups)
    def _(g):
        arrived(0, 0, g)
        for k in range(1, high_count):
            forward_copy(0, k, g).start()
        for k in range(1, high_count):
            arrived(k * 2 - 1, 1, g)
            forward_copy(1, k, g).start()

        @pl.loop(0, step)
        def _(j):
            couple_mode(g * step + j)

    tiles_load.wait()

    def near_mode(m):
        for r in range(row_tiles):
            total = None
            for slot in range(-1, shards - 1):
                dk, dl = (slot + 1) // 2, (slot + 1) % 2
                source = lax.rem(high + dk, high_count) * 2 + (low if dl == 0 else 1 - low)
                which = index_ref[m, r, source]
                picked = []
                for c in range(2):
                    if slot < 0:
                        block = extended[c, reach + m]
                    else:
                        block = gathered[slot, c, m]
                    chosen = block[:tile]
                    for t in range(1, points // tile):
                        chosen = lax.select(which == t, block[t * tile : (t + 1) * tile], chosen)
                    picked.append(chosen)
                k_r = tiles[m, r, source, 0]
                k_i = tiles[m, r, source, 1]
                left = jnp.concatenate(
                    [jnp.concatenate([k_r, -k_i], axis=1), jnp.concatenate([k_i, k_r], axis=1)], axis=0
                )
                product = jnp.dot(left, jnp.concatenate(picked, axis=0), preferred_element_type=F32)
                total = product if total is None else total + product
            rows = pl.ds(r * tile, tile)
            for c in range(2):
                value = 0.5 * extended[c, reach + m, rows, :].astype(F32)
                value = value + total[c * tile : (c + 1) * tile] + result[c, m, rows, :].astype(F32)
                result[c, m, rows, :] = value.astype(BF16)

    def out_copy(g):
        return pltpu.make_async_copy(result.at[:, part(g)], out_ref.at[:, part(g)], out_sems.at[g])

    @pl.loop(0, groups)
    def _(g):
        arrived(0, 1, g)
        for k in range(1, high_count):
            arrived(k * 2 - 1, 0, g)
            arrived(k * 2, 0, g)
            arrived(k * 2, 1, g)

        @pl.loop(0, step)
        def _(j):
            near_mode(g * step + j)

        out_copy(g).start()

    @pl.loop(0, groups)
    def _(g):
        for c in range(2):
            for k in range(high_count):
                own_copy(c, k, g).wait_send()
            for k in range(1, high_count):
                forward_copy(c, k, g).wait_send()
        out_copy(g).wait()

    @pl.when(has_right)
    def _():
        halo_copy(0).wait_send()

    @pl.when(has_left)
    def _():
        halo_copy(1).wait_send()


def apply_local(mode_devices, shard_count, density, kernel_tiles, tile_index, coupling, spread, liner):
    modes, points, rhs = density.shape[1:]
    band = coupling.shape[1]
    reach = band // 2
    groups = 8 if modes % 8 == 0 else modes
    step = modes // groups
    high_count = shard_count // 2
    dma = pltpu.SemaphoreType.DMA
    vmem = pl.BlockSpec(memory_space=pltpu.VMEM)
    cfg = (shard_count, groups, step, modes, reach, mode_devices)
    return pl.pallas_call(
        functools.partial(operator_kernel, cfg),
        out_shape=jax.ShapeDtypeStruct(density.shape, BF16),
        in_specs=[
            pl.BlockSpec(memory_space=pltpu.SMEM), vmem, vmem, vmem,
            pl.BlockSpec(memory_space=pl.ANY), pl.BlockSpec(memory_space=pl.ANY),
        ],
        out_specs=pl.BlockSpec(memory_space=pl.ANY),
        scratch_shapes=[
            pltpu.VMEM((2, modes + 2 * reach, points, rhs), BF16),
            pltpu.VMEM((shard_count - 1, 2, modes, points, rhs), BF16),
            pltpu.VMEM(kernel_tiles.shape, BF16),
            pltpu.VMEM(density.shape, BF16),
            pltpu.VMEM(coupling.shape, F32),
            pltpu.VMEM((128, points), F32),
            pltpu.VMEM((points, 128), F32),
            dma((2, high_count, groups)),
            dma((2, max(high_count - 1, 1), groups)),
            dma((shard_count - 1, 2, groups)),
            dma((2,)),
            dma((2,)),
            dma((2,)),
            dma((groups,)),
        ],
        compiler_params=pltpu.CompilerParams(
            collective_id=0, has_side_effects=True, vmem_limit_bytes=60 * MIB
        ),
    )(tile_index, spread.reshape(1, -1), liner.reshape(1, -1), coupling, density, kernel_tiles)


def solution(mesh):
    body = functools.partial(apply_local, mesh.shape["mode"], mesh.shape["blk"])
    return jax.shard_map(
        body,
        mesh=mesh,
        in_specs=(
            P(None, "mode", "blk", None),
            P("mode", "blk", None, None, None, None),
            P("mode", "blk", None),
            P(None, None, "mode", "blk"),
            P("blk"),
            P("blk"),
        ),
        out_specs=P(None, "mode", "blk", None),
        check_vma=False,
    )
```

time: 356 us -> 151 us (0.42)
  Pallas kernels: 0 us -> 144 us
  other arithmetic: 132 us -> 0 us
  matrix products: 94.1 us -> 0 us
  waiting for transfers between devices: 65.5 us -> 0 us
  local copies, waits for them, and re-layouts: 47.2 us -> 6.01 us
  between operations: 13.5 us -> 0.01 us
  starting transfers between devices: 3.7 us -> 0 us
    pallas_call x0 -> x1, Pallas kernels: none -> 144 us  [apply_local(): pl.pallas_call(functools.partial(operator_kernel, cfg), out_shape=jax.Sha...]
    dot_general x20 -> x0, matrix products: 94.1 us -> none  [the longest x4 66.9 us: one_shard(): jnp.einsum('mts,cmsqr->cmtqr', one_hot, shard_block, preferred_element_ty...]
    all_gather x1 -> x0, waiting for transfers between devices: 63.9 us -> none  [shards(): gathered = lax.all_gather(density, 'blk', axis=2, tiled=True)]
    another operation x2 -> x0, other arithmetic: 50.8 us -> none
    add x4 -> x0, other arithmetic: 36.5 us -> none  [one_shard(): return running + jnp.stack([real_part, imag_part])]
    convert_element_type x5 -> x0, other arithmetic: 34.9 us -> none  [the longest x2 26.9 us: couple_modes(): shifted = padded[:, offset:offset + mode_count].astype(jnp.float32)]
    dynamic_slice x8 -> x0, local copies, waits for them, and re-layouts: 21.5 us -> none  [the longest x4 18.7 us: one_shard(): lax.dynamic_slice_in_dim(gathered, position * point_count, point_count, 2)]
    squeeze x8 -> x0, local copies, waits for them, and re-layouts: 19.2 us -> none  [the longest x4 11.8 us: one_shard(): picked_tiles[0]]
  transfers between devices with their start and end apart: 3 -> 0, of which waited for: 2 -> 0; matrix products, arithmetic and copies ran while one was open for 25% -> 0% of each run, Pallas kernels for 0% -> 0%
where the time goes in v1:
time: 151 us; the launch traced here: 150 us
  Pallas kernels  144 us (95%)
  local copies, waits for them, and re-layouts  6.01 us (4%)
    pallas_call x1, Pallas kernels, apply_local(): pl.pallas_call(functools.partial(operator_kernel, cfg), out_shape=jax.Sha...  144 us
    unnamed x2, local copies, waits for them, and re-layouts  6.01 us

profile of v1, /device:TPU:0, one launch (start us, length us, event | category | flops | bytes accessed | tf_op | source)
XLA Modules:
  0.0 150.4 jit_solution(14229013598355205695)
XLA Ops:
  0.0 1.4 copy.7.index_ref
  1.4 144.4 %shard_map.64 = bf16[2,16,256,256]{3,2,1,0:T(8,128)(2,1)} custom-call(s32[16,2,4]{2,1,0:T(2,128)} %copy.7.index_ref, s32[1,256]{1,0:T(1,128)} %bitcast.2, s32[1,256]{1,0:T(1,128)} %bitcast.3, bf16[2,9,16,256]{3,2,1,0:T(8,128)(2,1)} %coupling_ref.1, bf16[2,16,256,256]{3,2,1,0:T(8,128)(2,1)} %density_ref.1, bf16[16,2,4,2,128,128]{5,4,3,2,1,0:T(8,128)(2,1)} %tiles_ref.1), custom_call_target="tpu_custom_call" | custom-call | tf_op jit(solution)/shard_map/pallas_call | solution.py:265
  145.8 4.6 %copy.9 = bf16[2,16,256,256]{3,2,1,0:T(8,128)(2,1)} copy(bf16[2,16,256,256]{3,2,1,0:T(8,128)(2,1)} %shard_map.64) | data formatting | bytes 8388608

commit v2 on v1

--- a/solution.py
+++ b/solution.py
@@ -14,9 +14,9 @@
 
 
 def operator_kernel(
-    cfg, index_ref, spread_ref, liner_ref, coupling_ref, density_ref, tiles_ref, out_ref,
-    extended, gathered, tiles, result, coupling32, raw, weights,
-    own_sems, forward_sems, arrive_sems, halo_send, halo_arrive, local_sems, out_sems,
+    cfg, index_ref, spread_ref, liner_ref, coupling_ref, density_ref, tiles_ref, result,
+    extended, gathered, tiles, coupling32, raw, weights,
+    own_sems, forward_sems, arrive_sems, halo_send, halo_arrive, local_sems,
 ):
     shards, groups, step, modes, reach, mode_devices = cfg
     high_count = shards // 2
@@ -193,7 +193,7 @@
             for slot in range(-1, shards - 1):
                 dk, dl = (slot + 1) // 2, (slot + 1) % 2
                 source = lax.rem(high + dk, high_count) * 2 + (low if dl == 0 else 1 - low)
-                which = index_ref[m, r, source]
+                which = index_ref[r, source, m]
                 picked = []
                 for c in range(2):
                     if slot < 0:
@@ -217,9 +217,6 @@
                 value = value + total[c * tile : (c + 1) * tile] + result[c, m, rows, :].astype(F32)
                 result[c, m, rows, :] = value.astype(BF16)
 
-    def out_copy(g):
-        return pltpu.make_async_copy(result.at[:, part(g)], out_ref.at[:, part(g)], out_sems.at[g])
-
     @pl.loop(0, groups)
     def _(g):
         arrived(0, 1, g)
@@ -231,8 +228,6 @@
         @pl.loop(0, step)
         def _(j):
             near_mode(g * step + j)
-
-        out_copy(g).start()
 
     @pl.loop(0, groups)
     def _(g):
@@ -241,7 +236,6 @@
                 own_copy(c, k, g).wait_send()
             for k in range(1, high_count):
                 forward_copy(c, k, g).wait_send()
-        out_copy(g).wait()
 
     @pl.when(has_right)
     def _():
@@ -264,17 +258,16 @@
     cfg = (shard_count, groups, step, modes, reach, mode_devices)
     return pl.pallas_call(
         functools.partial(operator_kernel, cfg),
-        out_shape=jax.ShapeDtypeStruct(density.shape, BF16),
+        out_shape=pltpu.VMEM(density.shape, BF16),
         in_specs=[
             pl.BlockSpec(memory_space=pltpu.SMEM), vmem, vmem, vmem,
-            pl.BlockSpec(memory_space=pl.ANY), pl.BlockSpec(memory_space=pl.ANY),
+            pl.BlockSpec(memory_space=pltpu.HBM), pl.BlockSpec(memory_space=pltpu.HBM),
         ],
-        out_specs=pl.BlockSpec(memory_space=pl.ANY),
+        out_specs=vmem,
         scratch_shapes=[
             pltpu.VMEM((2, modes + 2 * reach, points, rhs), BF16),
             pltpu.VMEM((shard_count - 1, 2, modes, points, rhs), BF16),
             pltpu.VMEM(kernel_tiles.shape, BF16),
-            pltpu.VMEM(density.shape, BF16),
             pltpu.VMEM(coupling.shape, F32),
             pltpu.VMEM((128, points), F32),
             pltpu.VMEM((points, 128), F32),
@@ -284,12 +277,11 @@
             dma((2,)),
             dma((2,)),
             dma((2,)),
-            dma((groups,)),
         ],
         compiler_params=pltpu.CompilerParams(
-            collective_id=0, has_side_effects=True, vmem_limit_bytes=60 * MIB
+            collective_id=0, has_side_effects=True, vmem_limit_bytes=56 * MIB
         ),
-    )(tile_index, spread.reshape(1, -1), liner.reshape(1, -1), coupling, density, kernel_tiles)
+    )(tile_index.transpose(1, 2, 0), spread.reshape(1, -1), liner.reshape(1, -1), coupling, density, kernel_tiles)
 
 
 def solution(mesh):

time: 151 us -> 146 us (0.967)
  local copies, waits for them, and re-layouts: 6.01 us -> 2.02 us
    unnamed x2 -> x1, local copies, waits for them, and re-layouts: 6.01 us -> 2.02 us
where the time goes in v2:
time: 146 us
  Pallas kernels  143 us (98%)
  local copies, waits for them, and re-layouts  2.02 us (1%)
    pallas_call x1, Pallas kernels, apply_local(): pl.pallas_call(functools.partial(operator_kernel, cfg), out_shape=pltpu.V...  143 us

profile of v2, /device:TPU:0, one launch (start us, length us, event | category | flops | bytes accessed | tf_op | source)
XLA Modules:
  0.0 145.5 jit_solution(13762000738438518638)
XLA Ops:
  0.0 143.5 %shard_map.64 = bf16[2,16,256,256]{3,2,1,0:T(8,128)(2,1)S(1)} custom-call(s32[2,4,16]{2,1,0:T(4,128)} %bitcast.3, s32[1,256]{1,0:T(1,128)} %bitcast.4, s32[1,256]{1,0:T(1,128)} %bitcast.5, bf16[2,9,16,256]{3,2,1,0:T(8,128)(2,1)} %coupling_ref.1, bf16[2,16,256,256]{3,2,1,0:T(8,128)(2,1)} %density_ref.1, bf16[16,2,4,2,128,128]{5,4,3,2,1,0:T(8,128)(2,1)} %tiles_ref.1), custom_call_target="tpu_custom_call" | custom-call | tf_op jit(solution)/shard_map/pallas_call | solution.py:259
  143.5 2.0 %copy.8 = bf16[2,16,256,256]{3,2,1,0:T(8,128)(2,1)} copy(bf16[2,16,256,256]{3,2,1,0:T(8,128)(2,1)S(1)} %shard_map.64) | data formatting | bytes 8388608

commit v3 on v2

--- a/solution.py
+++ b/solution.py
@@ -14,8 +14,8 @@
 
 
 def operator_kernel(
-    cfg, index_ref, spread_ref, liner_ref, coupling_ref, density_ref, tiles_ref, result,
-    extended, gathered, tiles, coupling32, raw, weights,
+    cfg, index_hbm, spread_ref, liner_ref, coupling_ref, density_ref, tiles_ref, result,
+    extended, gathered, tiles, coupling16, spread32, liner32, index_ref, coupling32, raw, weights,
     own_sems, forward_sems, arrive_sems, halo_send, halo_arrive, local_sems,
 ):
     shards, groups, step, modes, reach, mode_devices = cfg
@@ -87,9 +87,6 @@
         density_ref, extended.at[:, pl.ds(reach, modes)], local_sems.at[0]
     )
     tiles_load = pltpu.make_async_copy(tiles_ref, tiles, local_sems.at[1])
-    own_load.start()
-    tiles_load.start()
-
     barrier = pltpu.get_barrier_semaphore()
     pl.semaphore_signal(barrier, inc=1, device_id={"blk": partner})
     for k in range(1, high_count):
@@ -114,6 +111,12 @@
     def _():
         halo_copy(1).start()
 
+    small_loads = [
+        pltpu.make_async_copy(source, target, local_sems.at[2 + at])
+        for at, (source, target) in enumerate(
+            [(coupling_ref, coupling16), (spread_ref, spread32), (liner_ref, liner32), (index_hbm, index_ref)]
+        )
+    ]
     @pl.loop(0, groups)
     def _(g):
         own_copy(0, 0, g).start()
@@ -126,7 +129,13 @@
         for k in range(1, high_count):
             own_copy(0, k, g).start()
 
-    coupling32[...] = coupling_ref[...].astype(F32)
+    for load in small_loads:
+        load.start()
+    own_load.start()
+    tiles_load.start()
+    for load in small_loads:
+        load.wait()
+    coupling32[...] = coupling16[...].astype(F32)
     raw[...] = jnp.zeros_like(raw)
 
     @pl.when(jnp.logical_not(has_left))
@@ -148,8 +157,8 @@
         halo_copy(1).wait_recv()
 
     def couple_mode(m):
-        on_liner = liner_ref[...] == 1
-        reach_of = spread_ref[...]
+        on_liner = liner32[...] == 1
+        reach_of = spread32[...]
         for d in range(band):
             inside = jnp.where(on_liner & (reach_of >= abs(d - reach)), 1.0, 0.0).astype(F32)
             for c in range(2):
@@ -184,6 +193,14 @@
         @pl.loop(0, step)
         def _(j):
             couple_mode(g * step + j)
+
+    @pl.when(has_right)
+    def _():
+        halo_copy(0).wait_send()
+
+    @pl.when(has_left)
+    def _():
+        halo_copy(1).wait_send()
 
     tiles_load.wait()
 
@@ -219,31 +236,20 @@
 
     @pl.loop(0, groups)
     def _(g):
+        for c in range(2):
+            for k in range(high_count):
+                own_copy(c, k, g).wait_send()
         arrived(0, 1, g)
         for k in range(1, high_count):
             arrived(k * 2 - 1, 0, g)
             arrived(k * 2, 0, g)
             arrived(k * 2, 1, g)
+            for c in range(2):
+                forward_copy(c, k, g).wait_send()
 
         @pl.loop(0, step)
         def _(j):
             near_mode(g * step + j)
-
-    @pl.loop(0, groups)
-    def _(g):
-        for c in range(2):
-            for k in range(high_count):
-                own_copy(c, k, g).wait_send()
-            for k in range(1, high_count):
-                forward_copy(c, k, g).wait_send()
-
-    @pl.when(has_right)
-    def _():
-        halo_copy(0).wait_send()
-
-    @pl.when(has_left)
-    def _():
-        halo_copy(1).wait_send()
 
 
 def apply_local(mode_devices, shard_count, density, kernel_tiles, tile_index, coupling, spread, liner):
@@ -254,20 +260,24 @@
     step = modes // groups
     high_count = shard_count // 2
     dma = pltpu.SemaphoreType.DMA
+    hbm = pl.BlockSpec(memory_space=pltpu.HBM)
     vmem = pl.BlockSpec(memory_space=pltpu.VMEM)
     cfg = (shard_count, groups, step, modes, reach, mode_devices)
     return pl.pallas_call(
         functools.partial(operator_kernel, cfg),
         out_shape=pltpu.VMEM(density.shape, BF16),
         in_specs=[
-            pl.BlockSpec(memory_space=pltpu.SMEM), vmem, vmem, vmem,
-            pl.BlockSpec(memory_space=pltpu.HBM), pl.BlockSpec(memory_space=pltpu.HBM),
+            hbm, hbm, hbm, hbm, hbm, hbm,
         ],
         out_specs=vmem,
         scratch_shapes=[
             pltpu.VMEM((2, modes + 2 * reach, points, rhs), BF16),
             pltpu.VMEM((shard_count - 1, 2, modes, points, rhs), BF16),
             pltpu.VMEM(kernel_tiles.shape, BF16),
+            pltpu.VMEM(coupling.shape, BF16),
+            pltpu.VMEM((1, points), jnp.int32),
+            pltpu.VMEM((1, points), jnp.int32),
+            pltpu.SMEM((tile_index.shape[1], tile_index.shape[2], modes), jnp.int32),
             pltpu.VMEM(coupling.shape, F32),
             pltpu.VMEM((128, points), F32),
             pltpu.VMEM((points, 128), F32),
@@ -276,7 +286,7 @@
             dma((shard_count - 1, 2, groups)),
             dma((2,)),
             dma((2,)),
-            dma((2,)),
+            dma((6,)),
         ],
         compiler_params=pltpu.CompilerParams(
             collective_id=0, has_side_effects=True, vmem_limit_bytes=56 * MIB

time: 146 us -> 145 us (level)
  no operation moved by 1% of the time
where the time goes in v3:
time: 145 us; the launch traced here: 144 us
  Pallas kernels  142 us (98%)
  local copies, waits for them, and re-layouts  2.02 us (1%)
    pallas_call x1, Pallas kernels, apply_local(): pl.pallas_call(functools.partial(operator_kernel, cfg), out_shape=pltpu.V...  142 us

profile of v3, /device:TPU:0, one launch (start us, length us, event | category | flops | bytes accessed | tf_op | source)
XLA Modules:
  0.0 144.5 jit_solution(5910167578976597379)
XLA Ops:
  0.0 142.4 %shard_map.64 = bf16[2,16,256,256]{3,2,1,0:T(8,128)(2,1)S(1)} custom-call(s32[2,4,16]{2,1,0:T(4,128)} %bitcast.3, s32[1,256]{1,0:T(1,128)} %bitcast.4, s32[1,256]{1,0:T(1,128)} %bitcast.5, bf16[2,9,16,256]{3,2,1,0:T(8,128)(2,1)} %coupling_ref.1, bf16[2,16,256,256]{3,2,1,0:T(8,128)(2,1)} %density_ref.1, bf16[16,2,4,2,128,128]{5,4,3,2,1,0:T(8,128)(2,1)} %tiles_ref.1), custom_call_target="tpu_custom_call" | custom-call | tf_op jit(solution)/shard_map/pallas_call | solution.py:266
  142.4 2.0 %copy.8 = bf16[2,16,256,256]{3,2,1,0:T(8,128)(2,1)} copy(bf16[2,16,256,256]{3,2,1,0:T(8,128)(2,1)S(1)} %shard_map.64) | data formatting | bytes 8388608

commit v4 on v3

--- a/solution.py
+++ b/solution.py
@@ -256,7 +256,7 @@
     modes, points, rhs = density.shape[1:]
     band = coupling.shape[1]
     reach = band // 2
-    groups = 8 if modes % 8 == 0 else modes
+    groups = modes
     step = modes // groups
     high_count = shard_count // 2
     dma = pltpu.SemaphoreType.DMA

time: 145 us -> 145 us (level)
  no operation moved by 1% of the time
where the time goes in v4:
time: 145 us
  Pallas kernels  143 us (99%)
  local copies, waits for them, and re-layouts  2.02 us (1%)
    pallas_call x1, Pallas kernels, apply_local(): pl.pallas_call(functools.partial(operator_kernel, cfg), out_shape=pltpu.V...  143 us

profile of v4, /device:TPU:0, one launch (start us, length us, event | category | flops | bytes accessed | tf_op | source)
XLA Modules:
  0.0 144.8 jit_solution(5770861863246203495)
XLA Ops:
  0.0 142.8 %shard_map.64 = bf16[2,16,256,256]{3,2,1,0:T(8,128)(2,1)S(1)} custom-call(s32[2,4,16]{2,1,0:T(4,128)} %bitcast.3, s32[1,256]{1,0:T(1,128)} %bitcast.4, s32[1,256]{1,0:T(1,128)} %bitcast.5, bf16[2,9,16,256]{3,2,1,0:T(8,128)(2,1)} %coupling_ref.1, bf16[2,16,256,256]{3,2,1,0:T(8,128)(2,1)} %density_ref.1, bf16[16,2,4,2,128,128]{5,4,3,2,1,0:T(8,128)(2,1)} %tiles_ref.1), custom_call_target="tpu_custom_call" | custom-call | tf_op jit(solution)/shard_map/pallas_call | solution.py:266
  142.8 2.0 %copy.8 = bf16[2,16,256,256]{3,2,1,0:T(8,128)(2,1)} copy(bf16[2,16,256,256]{3,2,1,0:T(8,128)(2,1)S(1)} %shard_map.64) | data formatting | bytes 8388608
